TPU v7x, 32 devices: a whole 2x2x4 slice. The times are simulated.
32 devices in a mesh: groups: 2 (over y), seq: 4 (over z), dp: 2 (over x), sub: 2 (over core).
Axes of the slice: x: 2, y: 2, z: 4, core: 2. Of those that a mesh axis runs over, the one named last changes fastest.
Arguments:
- signal: bfloat16 [8, 2048, 512], P(('groups', 'dp', 'sub'), 'seq'), parts along dimension 0, may hold values from -6 to 6
- conv_weight: bfloat16 [512, 3, 1024], P(('dp', 'sub')), may hold values from -0.15625 to 0.15625
- proj_weight: bfloat16 [512, 512], P(('dp', 'sub')), may hold values from -0.25 to 0.25
- cotangent: bfloat16 [8, 2048, 512], P(('groups', 'dp', 'sub'), 'seq'), parts along dimension 0, may hold values from -6 to 6
Outputs:
- output: bfloat16 [8, 2048, 512], P(('groups', 'dp', 'sub'), 'seq'), parts along dimension 0
- grad_input: bfloat16 [8, 2048, 512], P(('groups', 'dp', 'sub'), 'seq'), parts along dimension 0
- grad_conv: float32 [1024, 3, 1024], P(('groups', 'dp', 'sub')), parts along dimension 0
- grad_proj: float32 [1024, 512], P(('groups', 'dp', 'sub')), parts along dimension 0
There are 2 independent parts, one for each index of `groups`. A program takes and returns all parts, laid end to end along the dimension named above; an argument that names none is the same for every part. Nothing has to cross between parts.
All inputs are finite; a program needn't handle non-finite values.
Results may differ from a plain program's by a relative error of at most 0.012.
Values may be sent and summed in bfloat16 or wider, within the bound.
A program may use at most 64 MiB of HBM per device.

v0:
```python
import math

import jax
import jax.numpy as jnp
from jax import lax
from jax.sharding import PartitionSpec as P

DILATION = 512


def passed_along(block, axis, distance):
    devices = range(lax.axis_size(axis))
    route = [(i - distance, i) for i in devices if i - distance in devices]
    return lax.ppermute(block, axis, route)


def relay_earlier(block, reach_blocks):
    blocks = [block]
    current = block
    for step_index in range(reach_blocks):
        current = passed_along(current, "seq", 1)
        blocks.append(current)
    return jnp.concatenate(blocks[::-1], axis=0)


def relay_later(block, reach_blocks):
    blocks = [block]
    current = block
    for step_index in range(reach_blocks):
        current = passed_along(current, "seq", -1)
        blocks.append(current)
    return jnp.concatenate(blocks, axis=0)


def local(signal, conv_weight, proj_weight, cotangent):
    signal_block = signal[0]
    upstream = cotangent[0]
    row_count, channels = signal_block.shape
    offsets = [tap_index * DILATION for tap_index in range(3)]
    reach_blocks = (2 * DILATION + row_count - 1) // row_count
    full_conv = lax.all_gather(conv_weight, ("dp", "sub"), axis=0, tiled=True)
    full_proj = lax.all_gather(proj_weight, ("dp", "sub"), axis=0, tiled=True)
    window = relay_earlier(signal_block, reach_blocks)
    base_row = reach_blocks * row_count
    taps = [window[base_row - offset : base_row - offset + row_count] for offset in offsets]
    preact = jnp.dot(taps[0], full_conv[:, 0, :], preferred_element_type=jnp.float32)
    for tap_index in range(1, 3):
        preact = preact + jnp.dot(
            taps[tap_index], full_conv[:, tap_index, :], preferred_element_type=jnp.float32
        )
    tanh_part = jnp.tanh(preact[:, :channels])
    gate_part = jax.nn.sigmoid(preact[:, channels:])
    gated = (tanh_part * gate_part).astype(jnp.bfloat16)
    output = (
        signal_block.astype(jnp.float32)
        + jnp.dot(gated, full_proj, preferred_element_type=jnp.float32)
    ).astype(jnp.bfloat16)
    transposed = (((1,), (1,)), ((), ()))
    grad_gated = lax.dot_general(
        upstream,
        lax.all_gather(proj_weight, ("dp", "sub"), axis=0, tiled=True),
        transposed,
        preferred_element_type=jnp.float32,
    )
    grad_pre = jnp.concatenate(
        [
            grad_gated * gate_part * (1.0 - tanh_part * tanh_part),
            grad_gated * tanh_part * gate_part * (1.0 - gate_part),
        ],
        axis=1,
    ).astype(jnp.bfloat16)
    ahead_window = relay_later(grad_pre, reach_blocks)
    futures = [ahead_window[offset : offset + row_count] for offset in offsets]
    panel = lax.all_gather(conv_weight, ("dp", "sub"), axis=0, tiled=True)
    summed = lax.dot_general(
        futures[0], panel[:, 0, :], transposed, preferred_element_type=jnp.float32
    )
    for tap_index in range(1, 3):
        summed = summed + lax.dot_general(
            futures[tap_index],
            panel[:, tap_index, :],
            transposed,
            preferred_element_type=jnp.float32,
        )
    grad_input = (upstream.astype(jnp.float32) + summed).astype(jnp.bfloat16)
    outer = (((0,), (0,)), ((), ()))
    terms = [
        lax.dot_general(taps[tap_index], grad_pre, outer, preferred_element_type=jnp.float32)
        for tap_index in range(3)
    ]
    conv_share = lax.psum_scatter(
        jnp.stack(terms, axis=1).astype(jnp.bfloat16),
        ("dp", "sub"),
        scatter_dimension=0,
        tiled=True,
    )
    proj_share = lax.psum_scatter(
        lax.dot_general(gated, upstream, outer, preferred_element_type=jnp.float32).astype(
            jnp.bfloat16
        ),
        ("dp", "sub"),
        scatter_dimension=0,
        tiled=True,
    )
    conv_total, proj_total = (
        lax.psum(conv_share, "seq").astype(jnp.float32),
        lax.psum(proj_share, "seq").astype(jnp.float32),
    )
    all_rows = row_count * lax.axis_size("seq") * lax.axis_size(("dp", "sub"))
    factor = 1.0 / math.sqrt(all_rows)
    return (output[None], grad_input[None], conv_total * factor, proj_total * factor)


def solution(mesh):
    placed = (
        P(("groups", "dp", "sub"), "seq", None),
        P(("dp", "sub"), None, None),
        P(("dp", "sub"), None),
        P(("groups", "dp", "sub"), "seq", None),
    )
    return jax.shard_map(
        local,
        mesh=mesh,
        in_specs=placed,
        out_specs=(
            P(("groups", "dp", "sub"), "seq", None),
            P(("groups", "dp", "sub"), "seq", None),
            P(("groups", "dp", "sub"), None, None),
            P(("groups", "dp", "sub"), None),
        ),
        check_vma=False,
    )
```

profile of v0, /device:TPU:0, one launch (start us, length us, event | category | flops | bytes accessed | tf_op | source)
XLA Modules:
  0.0 176.0 jit_solution(7137187538387217942)
XLA Ops:
  7.2 0.7 all-gather.2.cloned.1.call-update
  7.9 5.0 %collective-permute-start = (bf16[512,512]{1,0:T(8,128)(2,1)}, bf16[512,512]{1,0:T(8,128)(2,1)S(1)}, u32[]{:S(2)}, u32[]{:S(2)}) collective-permute-start(bf16[512,512]{1,0:T(8,128)(2,1)} %bitcast.57), channel_id=1, source_target_pairs={{0,4},{4,8},{8,12},{1,5},{5,9},{9,13},{2,6},{6,10},{10,14},{3,7},{... | collective-permute-start | bytes 1572872 | tf_op jit(solution)/shard_map/ppermute | solution.py:14
  12.9 7.4 %all_gather.9 = bf16[512,512]{1,0:T(8,128)(2,1)S(1)} all-gather(bf16[128,512]{1,0:T(8,128)(2,1)} %param.6), channel_id=1, replica_groups=mesh['groups'=2,'seq'=4,'dp'=2,'sub'=2] {'dp','sub'}, dimensions={0}, use_global_device_ids=true | all-gather | bytes 655360 | tf_op jit(solution)/shard_map/all_gather | solution.py:42
  20.3 4.1 %collective-permute-done = bf16[512,512]{1,0:T(8,128)(2,1)S(1)} collective-permute-done((bf16[512,512]{1,0:T(8,128)(2,1)}, bf16[512,512]{1,0:T(8,128)(2,1)S(1)}, u32[]{:S(2)}, u32[]{:S(2)}) %collective-permute-start) | collective-permute-done | bytes 524320 | tf_op jit(solution)/shard_map/ppermute | solution.py:14
  24.4 4.3 %collective-permute-start.1 = (bf16[512,512]{1,0:T(8,128)(2,1)S(1)}, bf16[512,512]{1,0:T(8,128)(2,1)S(1)}, u32[]{:S(2)}, u32[]{:S(2)}) collective-permute-start(bf16[512,512]{1,0:T(8,128)(2,1)S(1)} %collective-permute-done), channel_id=1, source_target_pairs={{0,4},{4,8},{8,12},{1,5},{5,9},{9,13},{2,6},{6,10},{10,14},{3,7},{... | collective-permute-start | bytes 1572872 | tf_op jit(solution)/shard_map/ppermute | solution.py:14
  28.7 12.2 %all-gather.2.cloned.1.call-done = bf16[512,3,1024]{2,0,1:T(8,128)(2,1)} async-done(((bf16[128,3,1024]{2,0,1:T(8,128)(2,1)}), bf16[512,3,1024]{2,0,1:T(8,128)(2,1)}) %all-gather.2.cloned.1.call-update) | async-done | bytes 3145744 | tf_op jit(solution)/shard_map/all_gather | solution.py:41
  40.8 2.2 %fusion.12 = f32[512,1024]{1,0:T(8,128)S(1)} fusion(bf16[512,3,1024]{2,0,1:T(8,128)(2,1)} %all-gather.2.cloned.1.call-done, bf16[1,512,512]{2,1,0:T(8,128)(2,1)} %param.4), kind=kOutput, calls=%fused_computation.31 | convolution fusion | flops 536870912 | bytes 3670016 | tf_op jit(solution)/shard_map/dot_general | solution.py:46
  43.2 0.7 fusion.13
  44.0 0.8 add_add_fusion
  45.0 1.7 multiply_convert_fusion.1
  46.7 0.7 fusion.1
  47.4 0.7 fusion.3
  48.2 0.7 fusion.2
  49.0 0.3 pad_maximum_fusion
  49.3 3.1 %copy.17 = bf16[512,3072]{1,0:T(8,128)(2,1)} copy(bf16[512,3072]{0,1:T(8,128)(2,1)S(1)} %bitcast.55) | data formatting | bytes 6291456
  52.4 1.0 copy-done.5
  53.6 1.1 pad_maximum_fusion.1
  54.7 1.3 collective-permute-start.2
  56.0 1.3 convolution_convert_fusion.3
  57.3 24.9 %collective-permute-done.2 = bf16[512,1024]{1,0:T(8,128)(2,1)} collective-permute-done((bf16[512,1024]{1,0:T(8,128)(2,1)}, bf16[512,1024]{1,0:T(8,128)(2,1)}, u32[]{:S(2)}, u32[]{:S(2)}) %collective-permute-start.2) | collective-permute-done | bytes 1048608 | tf_op jit(solution)/shard_map/ppermute | solution.py:14
  82.2 1.3 collective-permute-start.3
  83.5 2.6 %fusion.7 = bf16[1,512,512]{2,1,0:T(8,128)(2,1)} fusion(bf16[512,512]{1,0:T(8,128)(2,1)} %get-tuple-element.16, bf16[512,512]{1,0:T(8,128)(2,1)} %copy-done.3, bf16[1,512,512]{2,1,0:T(8,128)(2,1)} %param.4), kind=kOutput, calls=%fused_computation.17 | convolution fusion | flops 269221888 | bytes 2097152 | tf_op jit(solution)/shard_map/dot_general | solution.py:56
  86.1 4.4 %reduce-scatter.7.cloned.1.call-done = bf16[128,3072]{1,0:T(8,128)(2,1)} async-done(((bf16[512,3072]{1,0:T(8,128)(2,1)}), bf16[128,3072]{1,0:T(8,128)(2,1)}) %reduce-scatter.7.cloned.1.call-update) | async-done | bytes 786448
  90.5 2.3 %copy.18 = bf16[128,3072]{0,1:T(8,128)(2,1)} copy(bf16[128,3072]{1,0:T(8,128)(2,1)} %reduce-scatter.7.cloned.1.call-done) | data formatting | bytes 1572864
  92.8 22.1 %reduce-scatter.5.cloned.1.call-done = bf16[128,512]{1,0:T(8,128)(2,1)} async-done(((bf16[512,512]{1,0:T(8,128)(2,1)}), bf16[128,512]{1,0:T(8,128)(2,1)}) %reduce-scatter.5.cloned.1.call-update) | async-done | bytes 131088 | tf_op jit(solution)/shard_map/reduce_scatter | solution.py:97
  114.9 1.9 %fusion.11 = f32[512,512]{1,0:T(8,128)S(1)} fusion(bf16[512,3,1024]{2,0,1:T(8,128)(2,1)S(1)} %copy-done.1, bf16[512,512]{1,0:T(8,128)(2,1)} %copy-done.6, bf16[512,512]{1,0:T(8,128)(2,1)} %copy-done.4), kind=kOutput, calls=%fused_computation.30 | convolution fusion | flops 538968064 | bytes 3145728 | tf_op jit(solution)/shard_map/dot_general | solution.py:75
  116.9 2.0 %convolution_add_fusion.1 = f32[512,512]{1,0:T(8,128)S(1)} fusion(f32[512,512]{1,0:T(8,128)S(1)} %fusion.11, bf16[512,1024]{1,0:T(8,128)(2,1)} %collective-permute-done.2, bf16[512,3,1024]{2,0,1:T(8,128)(2,1)S(1)} %copy-done.1), kind=kOutput, calls=%fused_computation.8 | convolution fusion | flops 537133056 | bytes 4194304 | tf_op jit(solution)/shard_map/dot_general | solution.py:79
  118.9 2.8 %fusion.6 = bf16[1,512,512]{2,1,0:T(8,128)(2,1)} fusion(f32[512,512]{1,0:T(8,128)S(1)} %convolution_add_fusion.1, bf16[512,1024]{1,0:T(8,128)(2,1)} %collective-permute-done.3, bf16[512,3,1024]{2,0,1:T(8,128)(2,1)S(1)} %copy-done.1, bf16[1,512,512]{2,1,0:T(8,128)(2,1)S(1)} %copy-done.12), kind=kOutput, calls=%fused_computation.16 | convolution fusion | flops 537919488 | bytes 4194304 | tf_op jit(solution)/shard_map/dot_general | solution.py:79
  121.7 44.2 %all-reduce.3.cloned.1.call-done = (bf16[128,3,1024]{0,2,1:T(8,128)(2,1)}, bf16[128,512]{1,0:T(8,128)(2,1)}) async-done(((bf16[128,3,1024]{0,2,1:T(8,128)(2,1)}, bf16[128,512]{1,0:T(8,128)(2,1)}), (bf16[128,3,1024]{0,2,1:T(8,128)(2,1)}, bf16[128,512]{1,0:T(8,128)(2,1)})) %all-reduce.3.cloned.1.call-update) | async-done | bytes 917520 | tf_op jit(solution)/shard_map/psum | solution.py:106
  165.9 1.3 convert_multiply_fusion
  167.2 1.6 copy.13
  168.8 0.7 convert_multiply_fusion.1
  (34 shorter events, 0.8 us)
Async XLA Ops:
  7.2 33.7 %all-gather.2.cloned.1.call-start = ((), (), s32[]{:S(2)}) async-start(), calls=%async_computation.2 | async-start | bytes 3932160 | tf_op jit(solution)/shard_map/all_gather | solution.py:41
  7.9 82.6 %reduce-scatter.7.cloned.1.call-start = ((), (), s32[]{:S(2)}) async-start(), calls=%async_computation.4 | async-start | bytes 3932160
  7.9 16.4 %collective-permute-start = (bf16[512,512]{1,0:T(8,128)(2,1)}, bf16[512,512]{1,0:T(8,128)(2,1)S(1)}, u32[]{:S(2)}, u32[]{:S(2)}) collective-permute-start(bf16[512,512]{1,0:T(8,128)(2,1)} %bitcast.57), channel_id=1, source_target_pairs={{0,4},{4,8},{8,12},{1,5},{5,9},{9,13},{2,6},{6,10},{10,14},{3,7},{... | collective-permute-start | bytes 1572872 | tf_op jit(solution)/shard_map/ppermute | solution.py:14
  20.3 24.4 %copy-start.3 = (bf16[512,512]{1,0:T(8,128)(2,1)}, bf16[512,512]{1,0:T(8,128)(2,1)S(1)}, u32[]{:S(2)}) copy-start(bf16[512,512]{1,0:T(8,128)(2,1)S(1)} %all_gather.9) | copy-start | bytes 1572868
  24.4 19.6 %collective-permute-start.1 = (bf16[512,512]{1,0:T(8,128)(2,1)S(1)}, bf16[512,512]{1,0:T(8,128)(2,1)S(1)}, u32[]{:S(2)}, u32[]{:S(2)}) collective-permute-start(bf16[512,512]{1,0:T(8,128)(2,1)S(1)} %collective-permute-done), channel_id=1, source_target_pairs={{0,4},{4,8},{8,12},{1,5},{5,9},{9,13},{2,6},{6,10},{10,14},{3,7},{... | collective-permute-start | bytes 1572872 | tf_op jit(solution)/shard_map/ppermute | solution.py:14
  40.8 2.4 %copy-start = (bf16[512,3,1024]{2,0,1:T(8,128)(2,1)S(1)}, bf16[512,3,1024]{2,0,1:T(8,128)(2,1)}, u32[]{:S(2)}) copy-start(bf16[512,3,1024]{2,0,1:T(8,128)(2,1)} %all-gather.2.cloned.1.call-done) | copy-start | bytes 9437188
  43.9 1.0 copy-start.10
  45.0 1.7 copy-start.2
  46.7 1.5 copy-start.4
  46.7 1.5 copy-start.6
  52.4 1.0 copy-start.5
  52.4 1.2 copy-start.7
  52.4 3.6 %copy-start.8 = (bf16[512,512]{1,0:T(8,128)(2,1)S(1)}, bf16[512,512]{1,0:T(8,128)(2,1)}, u32[]{:S(2)}) copy-start(bf16[512,512]{1,0:T(8,128)(2,1)} %get-tuple-element.16) | copy-start | bytes 1572868
  52.4 3.6 %copy-start.11 = (bf16[1,512,512]{2,1,0:T(8,128)(2,1)S(1)}, bf16[1,512,512]{2,1,0:T(8,128)(2,1)}, u32[]{:S(2)}) copy-start(bf16[1,512,512]{2,1,0:T(8,128)(2,1)} %param.7) | copy-start | bytes 1572868
  52.4 62.5 %reduce-scatter.5.cloned.1.call-start = ((), (), s32[]{:S(2)}) async-start(), calls=%async_computation.3 | async-start | bytes 655360 | tf_op jit(solution)/shard_map/reduce_scatter | solution.py:97
  54.7 27.5 %collective-permute-start.2 = (bf16[512,1024]{1,0:T(8,128)(2,1)}, bf16[512,1024]{1,0:T(8,128)(2,1)}, u32[]{:S(2)}, u32[]{:S(2)}) collective-permute-start(bf16[512,1024]{1,0:T(8,128)(2,1)} %pad_maximum_fusion.1), channel_id=1, source_target_pairs={{4,0},{8,4},{12,8},{5,1},{9,5},{13,9},{6,2},{10,6},{14,10},{7,3},{... | collective-permute-start | bytes 3145736 | tf_op jit(solution)/shard_map/ppermute | solution.py:14
  57.3 57.6 %copy-start.1 = (bf16[512,3,1024]{2,0,1:T(8,128)(2,1)S(1)}, bf16[512,3,1024]{2,0,1:T(8,128)(2,1)}, u32[]{:S(2)}) copy-start(bf16[512,3,1024]{2,0,1:T(8,128)(2,1)} %all-gather.2.cloned.1.call-done) | copy-start | bytes 9437188
  57.3 108.6 %all-reduce.3.cloned.1.call-start = ((), (), s32[]{:S(2)}) async-start(), calls=%async_computation.5 | async-start | bytes 1835008 | tf_op jit(solution)/shard_map/psum | solution.py:106
  82.2 36.7 %collective-permute-start.3 = (bf16[512,1024]{1,0:T(8,128)(2,1)}, bf16[512,1024]{1,0:T(8,128)(2,1)}, u32[]{:S(2)}, u32[]{:S(2)}) collective-permute-start(bf16[512,1024]{1,0:T(8,128)(2,1)} %collective-permute-done.2), channel_id=1, source_target_pairs={{4,0},{8,4},{12,8},{5,1},{9,5},{13,9},{6,2},{10,6},{14,10},{7,3},{... | collective-permute-start | bytes 3145736 | tf_op jit(solution)/shard_map/ppermute | solution.py:14
  116.8 2.1 %copy-start.12 = (bf16[1,512,512]{2,1,0:T(8,128)(2,1)S(1)}, bf16[1,512,512]{2,1,0:T(8,128)(2,1)}, u32[]{:S(2)}) copy-start(bf16[1,512,512]{2,1,0:T(8,128)(2,1)} %param.7) | copy-start | bytes 1572868
  167.2 1.6 copy-start.9
Sparse Core Ops, SparseCore 0:
  9.6 31.2 all-gather.1
  52.5 37.9 reduce-scatter.6
  93.2 21.6 reduce-scatter.4
  117.7 48.1 all-reduce.2
where the time goes:
time: 177 us; the launch traced here: 176 us
  waiting for transfers between devices  113 us (64%)
  matrix products  18.3 us (10%)
  between operations  14 us (8%)
  starting transfers between devices  12 us (7%)
  local copies, waits for them, and re-layouts  8.45 us (5%)
  blocking collectives  7.38 us (4%)
  other arithmetic  3.45 us (2%)
    psum x1, waiting for transfers between devices, local(): lax.psum(conv_share, 'seq').astype(jnp.float32)  44.2 us
    ppermute x4, waiting for transfers between devices, passed_along(): return lax.ppermute(block, axis, route)  28.9 us
    reduce_scatter x1, waiting for transfers between devices, local(): lax.psum_scatter(lax.dot_general(gated, upstream, outer, preferred_elemen...  22.1 us
    all_gather x1, waiting for transfers between devices, local(): full_conv = lax.all_gather(conv_weight, ('dp', 'sub'), axis=0, tiled=True)  12.2 us
    ppermute x4, starting transfers between devices, passed_along(): return lax.ppermute(block, axis, route)  11.8 us
    unnamed x29, local copies, waits for them, and re-layouts  8.45 us
    all_gather x1, blocking collectives, local(): full_proj = lax.all_gather(proj_weight, ('dp', 'sub'), axis=0, tiled=True)  7.38 us
    unnamed x5, waiting for transfers between devices  5.17 us
  transfers between devices with their start and end apart: 8, of which 6 were waited for; matrix products, arithmetic and copies ran while one was open for 10% of the time, Pallas kernels for 0%

commit v1 on v0

v1 whole, which is shorter than its diff:
```python
import functools
import math

import jax
import jax.numpy as jnp
from jax import lax
from jax.experimental import pallas as pl
from jax.experimental.pallas import tpu as pltpu
from jax.sharding import PartitionSpec as P

DILATION = 512
TAPS = 3
PIECES = 4
CHUNKS = 2
MESH = pl.DeviceIdType.MESH
F32 = jnp.float32
BF16 = jnp.bfloat16
NN = (((1,), (0,)), ((), ()))
NT = (((1,), (1,)), ((), ()))


def mm(a, b, dims=NN):
    return lax.dot_general(a, b, dims, preferred_element_type=F32)


def layer_kernel(
    sizes, factor,
    sig, cw, pw, cot,
    out, gin, gconv, gproj,
    sig1, sig2, sigt, gatedt, w, wp, gp, gated,
    p2in, p1in, p2out, p1out,
    grads, half_in, x_out, x_in, share, z_out, z_below, z_above, total,
    halo_s, halo_r, wx_s, wx_r, wy_s, wy_r, wc_s, wc_r,
    p_s, p_r, c_s, c_r, x_s, x_r, zb_s, zb_r, za_s, za_r, tu_s, td_s, t_r,
):
    ny, nz, nx, nc = sizes
    h, z, d, c = (lax.axis_index(name) for name in ("groups", "seq", "dp", "sub"))
    rows, chans = sig.shape
    part = cw.shape[1]
    cut = part // ny
    step = rows // CHUNKS
    reduce_time = nz == PIECES
    below, above = z > 0, z < nz - 1

    def copy(src, dst, send, recv, **where):
        return pltpu.make_async_remote_copy(
            src_ref=src, dst_ref=dst, send_sem=send, recv_sem=recv,
            device_id=where, device_id_type=MESH,
        )

    barrier = pltpu.get_barrier_semaphore()

    def greet(**where):
        pl.semaphore_signal(barrier, inc=1, device_id=where, device_id_type=MESH)

    @pl.when(below)
    def _():
        greet(seq=z - 1)

    @pl.when(above)
    def _():
        greet(seq=z + 1)

    for o in range(1, nx):
        greet(dp=lax.rem(d + o, nx))
    greet(sub=1 - c)
    greet(groups=1 - h)
    pl.semaphore_wait(
        barrier, (nx - 1) + 2 + below.astype(jnp.int32) + above.astype(jnp.int32)
    )

    def rows_of(j):
        return pl.ds(j * step, step)

    own_halo = [
        copy(sig.at[rows_of(j)], sig1.at[rows_of(j)], halo_s.at[0, j], halo_r.at[0, j], seq=z + 1)
        for j in range(CHUNKS)
    ]
    far_halo = [
        copy(sig1.at[rows_of(j)], sig2.at[rows_of(j)], halo_s.at[1, j], halo_r.at[1, j], seq=z + 1)
        for j in range(CHUNKS)
    ]

    @pl.when(above)
    def _():
        for j in range(CHUNKS):
            own_halo[j].start()

    def shard(k):
        return cw.at[k] if k < TAPS else pw

    def full(k, at, length):
        at = pl.ds(pl.multiple_of(at, 16), length)
        return w.at[k, at] if k < TAPS else wp.at[at]

    def base(dp_index):
        return (dp_index * nc + c) * part

    mine = base(d)
    wx, wy, wc = {}, {}, {}
    for k in range(TAPS + 1):
        for o in range(1, nx):
            wx[k, o] = copy(
                shard(k).at[pl.ds(pl.multiple_of(h * cut, 16), cut)], full(k, mine + h * cut, cut),
                wx_s.at[k, o], wx_r.at[k, o], dp=lax.rem(d + o, nx),
            )
            wx[k, o].start()
    for k in range(TAPS + 1):
        wc[k, 0, 0] = copy(
            shard(k), full(k, mine, part), wc_s.at[k, 0, 0], wc_r.at[k, 0, 0], sub=1 - c
        )
        wc[k, 0, 0].start()
    at_mine = pl.ds(pl.multiple_of(mine, 16), part)
    for k in range(TAPS):
        w[k, at_mine] = cw[k]
    wp[at_mine] = pw[...]

    @pl.when(z == 0)
    def _():
        sig1[...] = jnp.zeros_like(sig1)

    @pl.when(z < 2)
    def _():
        sig2[...] = jnp.zeros_like(sig2)

    @pl.when(z == nz - 1)
    def _():
        p2in[...] = jnp.zeros_like(p2in)
        p1in[...] = jnp.zeros_like(p1in)

    def pass_halo(j):
        @pl.when(below)
        def _():
            own_halo[j].wait_recv()

        @pl.when(below & above)
        def _():
            far_halo[j].start()

    for k in range(TAPS + 1):
        for o in range(1, nx):
            wx[k, o].wait_recv()
            region = full(k, base(lax.rem(d - o + nx, nx)) + h * cut, cut)
            wy[k, o] = copy(region, region, wy_s.at[k, o], wy_r.at[k, o], groups=1 - h)
            wy[k, o].start()
            wc[k, o, 0] = copy(region, region, wc_s.at[k, o, 0], wc_r.at[k, o, 0], sub=1 - c)
            wc[k, o, 0].start()
        if k < CHUNKS:
            pass_halo(k)
    sigt[0] = sig[...].T
    for k in range(TAPS + 1):
        for o in range(1, nx):
            wy[k, o].wait_recv()
            region = full(k, base(lax.rem(d - o + nx, nx)) + (1 - h) * cut, cut)
            wc[k, o, 1] = copy(region, region, wc_s.at[k, o, 1], wc_r.at[k, o, 1], sub=1 - c)
            wc[k, o, 1].start()
    for item in wc.values():
        item.wait_recv()

    p2_copy = [
        copy(p2out.at[rows_of(j)], p2in.at[rows_of(j)], p_s.at[0, j], p_r.at[0, j], seq=z - 1)
        for j in range(CHUNKS)
    ]
    p1_copy = [
        copy(p1out.at[rows_of(j)], p1in.at[rows_of(j)], p_s.at[1, j], p_r.at[1, j], seq=z - 1)
        for j in range(CHUNKS)
    ]
    tile = 256
    for j in range(CHUNKS):
        r = rows_of(j)

        @pl.when(z > 1)
        def _():
            far_halo[j].wait_recv()

        def tile_body(n, carry):
            t_cols = pl.ds(pl.multiple_of(n * tile, tile), tile)
            g_cols = pl.ds(pl.multiple_of(chans + n * tile, tile), tile)
            tanh_pre = mm(sig[r], w[0, :, t_cols]) + mm(sig1[r], w[1, :, t_cols])
            tanh_pre = tanh_pre + mm(sig2[r], w[2, :, t_cols])
            gate_pre = mm(sig[r], w[0, :, g_cols]) + mm(sig1[r], w[1, :, g_cols])
            gate_pre = gate_pre + mm(sig2[r], w[2, :, g_cols])
            grad_gated = mm(cot[r], wp[t_cols, :], NT)
            tanh_part = jnp.tanh(tanh_pre)
            gate_part = jax.nn.sigmoid(gate_pre)
            g = (tanh_part * gate_part).astype(BF16)
            gated[r, t_cols] = g
            gatedt[t_cols, r] = g.T
            gp[r, t_cols] = (grad_gated * gate_part * (1.0 - tanh_part * tanh_part)).astype(BF16)
            gp[r, g_cols] = (grad_gated * tanh_part * gate_part * (1.0 - gate_part)).astype(BF16)
            return carry

        lax.fori_loop(0, chans // tile, tile_body, 0)

        @pl.when(below)
        def _():
            p2out[r] = mm(gp[r], w[2], NT).astype(BF16)
            p2_copy[j].start()

    sigt[1] = sig1[...].T
    sigt[2] = sig2[...].T

    order = (3, 0, 2, 1)
    conv_cols = 2 * chans // PIECES
    proj_cols = chans // PIECES
    c_copy, x_copy = {}, {}
    for q in order:
        for k in range(TAPS):
            grads[q, :, k * conv_cols:(k + 1) * conv_cols] = mm(
                sigt[k], gp[:, q * conv_cols:(q + 1) * conv_cols]
            ).astype(BF16)
        grads[q, :, TAPS * conv_cols:] = mm(
            gatedt[...], cot[:, q * proj_cols:(q + 1) * proj_cols]
        ).astype(BF16)
        for o in range(nx):
            e = lax.rem(d + o, nx)
            theirs = pl.ds(pl.multiple_of((e * nc + 1 - c) * part, 16), part)
            c_copy[q, o] = copy(
                grads.at[q, theirs], half_in.at[q, o], c_s.at[q, o], c_r.at[q, o], sub=1 - c
            )
            c_copy[q, o].start()

    for q in order:
        for o in list(range(1, nx)) + [0]:
            c_copy[q, o].wait_recv()
            e = lax.rem(d + o, nx)
            ours = pl.ds(pl.multiple_of(base(e), 16), part)
            summed = grads[q, ours].astype(F32) + half_in[q, o].astype(F32)
            if o == 0:
                share[q] = summed
            else:
                x_out[q, o] = summed.astype(BF16)
                x_copy[q, o] = copy(
                    x_out.at[q, o], x_in.at[q, o], x_s.at[q, o], x_r.at[q, o], dp=e
                )
                x_copy[q, o].start()

    for j in range(CHUNKS):
        r = rows_of(j)

        @pl.when(above)
        def _():
            p2_copy[j].wait_recv()

        @pl.when(below)
        def _():
            p1out[r] = (mm(gp[r], w[1], NT) + p2in[r].astype(F32)).astype(BF16)
            p1_copy[j].start()

    for j in range(CHUNKS):
        r = rows_of(j)
        out[r] = (sig[r].astype(F32) + mm(gated[r], wp[...])).astype(BF16)
    for j in range(CHUNKS):
        r = rows_of(j)
        local_sum = cot[r].astype(F32) + mm(gp[r], w[0], NT)

        @pl.when(above)
        def _():
            p1_copy[j].wait_recv()

        gin[r] = (local_sum + p1in[r].astype(F32)).astype(BF16)

    def take_x(q):
        for o in range(1, nx):
            x_copy[q, o].wait_recv()
            share[q] += x_in[q, o].astype(F32)

    def write_out(q, values):
        for k in range(TAPS):
            gconv[k, :, q * conv_cols:(q + 1) * conv_cols] = values[
                :, k * conv_cols:(k + 1) * conv_cols
            ]
        gproj[:, q * proj_cols:(q + 1) * proj_cols] = values[:, TAPS * conv_cols:]

    if reduce_time:
        up = [
            copy(z_out.at[q], z_below.at[q], zb_s.at[q], zb_r.at[q], seq=z + 1)
            for q in range(PIECES)
        ]
        down = [
            copy(z_out.at[q], z_above.at[q], za_s.at[q], za_r.at[q], seq=z - 1)
            for q in range(PIECES)
        ]

        def send_up(q):
            @pl.when(z < q)
            def _():
                @pl.when(below)
                def _():
                    up[q].wait_recv()
                    z_out[q] = (share[q] + z_below[q].astype(F32)).astype(BF16)

                @pl.when(z == 0)
                def _():
                    z_out[q] = share[q].astype(BF16)

                up[q].start()

        def send_down(q):
            @pl.when(z > q)
            def _():
                @pl.when(above)
                def _():
                    down[q].wait_recv()
                    z_out[q] = (share[q] + z_above[q].astype(F32)).astype(BF16)

                @pl.when(z == nz - 1)
                def _():
                    z_out[q] = share[q].astype(BF16)

                down[q].start()

        take_x(3)
        send_up(3)
        take_x(0)
        send_down(0)
        take_x(2)
        send_up(2)
        take_x(1)
        send_down(1)
        send_up(1)
        send_down(2)

        def total_up(q):
            return copy(total.at[q], total.at[q], tu_s.at[q], t_r.at[q], seq=z + 1)

        def total_down(q):
            return copy(total.at[q], total.at[q], td_s.at[q], t_r.at[q], seq=z - 1)

        for q in range(PIECES):
            @pl.when(z == q)
            def _():
                if q > 0:
                    up[q].wait_recv()
                    share[q] += z_below[q].astype(F32)
                if q < nz - 1:
                    down[q].wait_recv()
                    share[q] += z_above[q].astype(F32)
                total[q] = share[q].astype(BF16)
                if q < nz - 1:
                    total_up(q).start()
                if q > 0:
                    total_down(q).start()

        for distance in range(1, nz):
            @pl.when(z >= distance)
            def _():
                q = z - distance
                total_up(q).wait_recv()

                @pl.when(above)
                def _():
                    total_up(q).start()

            @pl.when(z + distance <= nz - 1)
            def _():
                q = z + distance
                total_down(q).wait_recv()

                @pl.when(below)
                def _():
                    total_down(q).start()

        for q in range(PIECES):
            write_out(q, total[q].astype(F32) * factor)

        for q in range(PIECES):
            @pl.when(z < q)
            def _():
                up[q].wait_send()

            @pl.when(z > q)
            def _():
                down[q].wait_send()

            @pl.when((z >= q) & above)
            def _():
                total_up(q).wait_send()

            @pl.when((z <= q) & below)
            def _():
                total_down(q).wait_send()
    else:
        for q in order:
            take_x(q)
            write_out(q, share[q])

    for item in (
        list(wx.values()) + list(wy.values()) + list(wc.values())
        + list(c_copy.values()) + list(x_copy.values())
    ):
        item.wait_send()

    @pl.when(above)
    def _():
        for j in range(CHUNKS):
            own_halo[j].wait_send()

    @pl.when(below & above)
    def _():
        for j in range(CHUNKS):
            far_halo[j].wait_send()

    @pl.when(below)
    def _():
        for j in range(CHUNKS):
            p2_copy[j].wait_send()
            p1_copy[j].wait_send()


def local(sizes, signal, conv_weight, proj_weight, cotangent):
    ny, nz, nx, nc = sizes
    rows, chans = signal.shape[1:]
    assert rows == DILATION and nc == 2 and ny == 2 and signal.shape[0] == 1
    part = conv_weight.shape[0]
    factor = 1.0 / math.sqrt(rows * nz * nx * nc)
    width = (TAPS * 2 * chans + chans) // PIECES
    dma = pltpu.SemaphoreType.DMA
    vmem = pltpu.VMEM
    block = vmem((rows, chans), BF16)
    piece = vmem((PIECES, part, width), BF16)
    scratch = [
        block, block,
        vmem((TAPS, chans, rows), BF16), vmem((chans, rows), BF16),
        vmem((TAPS, chans, 2 * chans), BF16), block, vmem((rows, 2 * chans), BF16), block,
        block, block, block, block,
        vmem((PIECES, chans, width), BF16),
        vmem((PIECES, nx, part, width), BF16),
        vmem((PIECES, nx, part, width), BF16),
        vmem((PIECES, nx, part, width), BF16),
        vmem((PIECES, part, width), F32),
        piece, piece, piece, piece,
    ] + [dma((2, CHUNKS))] * 2 + [dma((TAPS + 1, nx))] * 4 + [dma((TAPS + 1, nx, 2))] * 2 \
        + [dma((2, CHUNKS))] * 2 + [dma((PIECES, nx))] * 4 + [dma((PIECES,))] * 7
    spec = pl.BlockSpec(memory_space=pltpu.VMEM)
    output, grad_input, conv, proj = pl.pallas_call(
        functools.partial(layer_kernel, sizes, factor),
        out_shape=(
            jax.ShapeDtypeStruct((rows, chans), BF16),
            jax.ShapeDtypeStruct((rows, chans), BF16),
            jax.ShapeDtypeStruct((TAPS, part, 2 * chans), F32),
            jax.ShapeDtypeStruct((part, chans), F32),
        ),
        in_specs=[spec] * 4,
        out_specs=(spec,) * 4,
        scratch_shapes=scratch,
        compiler_params=pltpu.CompilerParams(
            collective_id=0, has_side_effects=True, vmem_limit_bytes=48 * 1024 * 1024
        ),
        cost_estimate=pl.CostEstimate(
            flops=22 * rows * chans * chans, bytes_accessed=8 << 20, transcendentals=2 * rows * chans
        ),
    )(signal[0], jnp.swapaxes(conv_weight, 0, 1), proj_weight, cotangent[0])
    conv = jnp.swapaxes(conv, 0, 1)
    if nz != PIECES:
        conv, proj = lax.psum((conv, proj), "seq")
        conv, proj = conv * factor, proj * factor
    return output[None], grad_input[None], conv, proj


def solution(mesh):
    sizes = tuple(mesh.shape[name] for name in ("groups", "seq", "dp", "sub"))
    rows_split = P(("groups", "dp", "sub"), "seq", None)
    return jax.shard_map(
        functools.partial(local, sizes),
        mesh=mesh,
        in_specs=(rows_split, P(("dp", "sub"), None, None), P(("dp", "sub"), None), rows_split),
        out_specs=(
            rows_split,
            rows_split,
            P(("groups", "dp", "sub"), None, None),
            P(("groups", "dp", "sub"), None),
        ),
        check_vma=False,
    )
```

time: 177 us -> 101 us (0.57)
  waiting for transfers between devices: 113 us -> 0 us
  Pallas kernels: 0 us -> 92.5 us
  matrix products: 18.3 us -> 0 us
  between operations: 14 us -> 0.65 us
  starting transfers between devices: 12 us -> 0 us
  blocking collectives: 7.38 us -> 0 us
  other arithmetic: 3.45 us -> 0 us
    pallas_call x0 -> x1, Pallas kernels: none -> 92.5 us  [local(): pl.pallas_call(functools.partial(layer_kernel, sizes, factor), out_shape=...]
    psum x1 -> x0, waiting for transfers between devices: 44.2 us -> none  [local(): lax.psum(conv_share, 'seq').astype(jnp.float32)]
    ppermute x4 -> x0, waiting for transfers between devices: 28.9 us -> none  [passed_along(): return lax.ppermute(block, axis, route)]
    reduce_scatter x1 -> x0, waiting for transfers between devices: 22.1 us -> none  [local(): lax.psum_scatter(lax.dot_general(gated, upstream, outer, preferred_elemen...]
    dot_general x12 -> x0, matrix products: 18.3 us -> none  [the longest x2 4.79 us: local(): lax.dot_general(futures[tap_index], panel[:, tap_index, :], transposed, p...]
    all_gather x1 -> x0, waiting for transfers between devices: 12.2 us -> none  [local(): full_conv = lax.all_gather(conv_weight, ('dp', 'sub'), axis=0, tiled=True)]
    ppermute x4 -> x0, starting transfers between devices: 11.8 us -> none  [passed_along(): return lax.ppermute(block, axis, route)]
    all_gather x1 -> x0, blocking collectives: 7.38 us -> none  [local(): full_proj = lax.all_gather(proj_weight, ('dp', 'sub'), axis=0, tiled=True)]
  transfers between devices with their start and end apart: 8 -> 0, of which waited for: 6 -> 0; matrix products, arithmetic and copies ran while one was open for 10% -> 0% of each run, Pallas kernels for 0% -> 0%
where the time goes in v1:
time: 101 us
  Pallas kernels  92.5 us (92%)
  local copies, waits for them, and re-layouts  7.54 us (7%)
    pallas_call x1, Pallas kernels, local(): pl.pallas_call(functools.partial(layer_kernel, sizes, factor), out_shape=...  92.5 us
    unnamed x12, local copies, waits for them, and re-layouts  7.54 us

profile of v1, /device:TPU:0, one launch (start us, length us, event | category | flops | bytes accessed | tf_op | source)
XLA Modules:
  0.0 100.7 jit_solution(4371745740693058784)
XLA Ops:
  0.6 0.0 copy-start
  0.6 1.1 %copy-done = bf16[128,3,1024]{2,0,1:T(8,128)(2,1)S(1)} copy-done((bf16[128,3,1024]{2,0,1:T(8,128)(2,1)S(1)}, bf16[128,3,1024]{2,0,1:T(8,128)(2,1)}, u32[]{:S(2)}) %copy-start) | copy-done | bytes 786456
  1.8 0.0 copy-start.1
  1.8 1.0 %copy-done.1 = bf16[1,512,512]{2,1,0:T(8,128)(2,1)S(1)} copy-done((bf16[1,512,512]{2,1,0:T(8,128)(2,1)S(1)}, bf16[1,512,512]{2,1,0:T(8,128)(2,1)}, u32[]{:S(2)}) %copy-start.1) | copy-done | bytes 524312
  2.8 0.0 copy-start.2
  2.8 1.0 %copy-done.2 = bf16[1,512,512]{2,1,0:T(8,128)(2,1)S(1)} copy-done((bf16[1,512,512]{2,1,0:T(8,128)(2,1)S(1)}, bf16[1,512,512]{2,1,0:T(8,128)(2,1)}, u32[]{:S(2)}) %copy-start.2) | copy-done | bytes 524312
  3.9 0.0 copy-start.3
  3.9 0.9 copy-done.3
  4.8 92.5 %shard_map.75 = (bf16[512,512]{1,0:T(8,128)(2,1)S(1)}, bf16[512,512]{1,0:T(8,128)(2,1)S(1)}, f32[3,128,1024]{2,1,0:T(8,128)S(1)}, f32[128,512]{1,0:T(8,128)S(1)}) custom-call(bf16[512,512]{1,0:T(8,128)(2,1)S(1)} %bitcast.10, bf16[3,128,1024]{2,1,0:T(8,128)(2,1)S(1)} %bitcast.9, bf16[128,512]{1,0:T(8,128)(2,1)S(1)} %copy-done.3, bf16[512,512]{1,0:T(8,128)(2,1)S(1)} %bitcast.11), custom_call_target="tpu_custom_call" | custom-call | flops 2952790016 | bytes 8388608 | tf_op jit(solution)/shard_map/pallas_call | solution.py:436
  97.2 0.8 copy.12
  98.0 0.8 copy.13
  98.8 1.1 %copy.14 = f32[128,3,1024]{2,0,1:T(8,128)} copy(f32[128,3,1024]{2,0,1:T(8,128)S(1)} %bitcast.6) | data formatting | bytes 3145728
  100.0 0.7 copy.15
Async XLA Ops:
  0.6 1.1 %copy-start = (bf16[128,3,1024]{2,0,1:T(8,128)(2,1)S(1)}, bf16[128,3,1024]{2,0,1:T(8,128)(2,1)}, u32[]{:S(2)}) copy-start(bf16[128,3,1024]{2,0,1:T(8,128)(2,1)} %param.5) | copy-start | bytes 2359300
  1.8 1.0 %copy-start.1 = (bf16[1,512,512]{2,1,0:T(8,128)(2,1)S(1)}, bf16[1,512,512]{2,1,0:T(8,128)(2,1)}, u32[]{:S(2)}) copy-start(bf16[1,512,512]{2,1,0:T(8,128)(2,1)} %param.4) | copy-start | bytes 1572868
  2.8 1.0 %copy-start.2 = (bf16[1,512,512]{2,1,0:T(8,128)(2,1)S(1)}, bf16[1,512,512]{2,1,0:T(8,128)(2,1)}, u32[]{:S(2)}) copy-start(bf16[1,512,512]{2,1,0:T(8,128)(2,1)} %param.7) | copy-start | bytes 1572868
  3.9 0.9 copy-start.3

commit v2 on v1

--- a/solution.py
+++ b/solution.py
@@ -11,7 +11,11 @@
 DILATION = 512
 TAPS = 3
 PIECES = 4
-CHUNKS = 2
+CHUNKS = 4
+OWE_LAG = 2
+HALVES = 4
+LAG_TOTAL = 2
+LAG_ON = 5
 MESH = pl.DeviceIdType.MESH
 F32 = jnp.float32
 BF16 = jnp.bfloat16
@@ -25,13 +29,13 @@
 
 def layer_kernel(
     sizes, factor,
-    sig, cw, pw, cot,
+    sig_hbm, cw, pw, cot_hbm,
     out, gin, gconv, gproj,
-    sig1, sig2, sigt, gatedt, w, wp, gp, gated,
+    sig, cot, gin_sum, sig1, sig2, sigt, gatedt, w, wp, gp, gated,
     p2in, p1in, p2out, p1out,
     grads, half_in, x_out, x_in, share, z_out, z_below, z_above, total,
     halo_s, halo_r, wx_s, wx_r, wy_s, wy_r, wc_s, wc_r,
-    p_s, p_r, c_s, c_r, x_s, x_r, zb_s, zb_r, za_s, za_r, tu_s, td_s, t_r,
+    p_s, p_r, c_s, c_r, x_s, x_r, zb_s, zb_r, za_s, za_r, tu_s, td_s, t_r, local_s,
 ):
     ny, nz, nx, nc = sizes
     h, z, d, c = (lax.axis_index(name) for name in ("groups", "seq", "dp", "sub"))
@@ -48,6 +52,15 @@
             device_id=where, device_id_type=MESH,
         )
 
+    part_at = pl.ds(pl.multiple_of((d * nc + c) * part, 16), part)
+    staged = [
+        pltpu.make_async_copy(sig_hbm, sig, local_s.at[0]),
+        pltpu.make_async_copy(cw, w.at[:, part_at], local_s.at[1]),
+        pltpu.make_async_copy(pw, wp.at[part_at], local_s.at[2]),
+        pltpu.make_async_copy(cot_hbm, cot, local_s.at[3]),
+    ]
+    for item in staged:
+        item.start()
     barrier = pltpu.get_barrier_semaphore()
 
     def greet(**where):
@@ -73,7 +86,7 @@
         return pl.ds(j * step, step)
 
     own_halo = [
-        copy(sig.at[rows_of(j)], sig1.at[rows_of(j)], halo_s.at[0, j], halo_r.at[0, j], seq=z + 1)
+        copy(sig_hbm.at[rows_of(j)], sig1.at[rows_of(j)], halo_s.at[0, j], halo_r.at[0, j], seq=z + 1)
         for j in range(CHUNKS)
     ]
     far_halo = [
@@ -110,10 +123,6 @@
             shard(k), full(k, mine, part), wc_s.at[k, 0, 0], wc_r.at[k, 0, 0], sub=1 - c
         )
         wc[k, 0, 0].start()
-    at_mine = pl.ds(pl.multiple_of(mine, 16), part)
-    for k in range(TAPS):
-        w[k, at_mine] = cw[k]
-    wp[at_mine] = pw[...]
 
     @pl.when(z == 0)
     def _():
@@ -147,6 +156,8 @@
             wc[k, o, 0].start()
         if k < CHUNKS:
             pass_halo(k)
+    for item in staged:
+        item.wait()
     sigt[0] = sig[...].T
     for k in range(TAPS + 1):
         for o in range(1, nx):
@@ -165,6 +176,18 @@
         copy(p1out.at[rows_of(j)], p1in.at[rows_of(j)], p_s.at[1, j], p_r.at[1, j], seq=z - 1)
         for j in range(CHUNKS)
     ]
+    def owe_next(j):
+        r = rows_of(j)
+
+        @pl.when(below & above)
+        def _():
+            p2_copy[j].wait_recv()
+
+        @pl.when(below)
+        def _():
+            p1out[r] = (mm(gp[r], w[1], NT) + p2in[r].astype(F32)).astype(BF16)
+            p1_copy[j].start()
+
     tile = 256
     for j in range(CHUNKS):
         r = rows_of(j)
@@ -192,19 +215,23 @@
 
         lax.fori_loop(0, chans // tile, tile_body, 0)
 
-        @pl.when(below)
+        @pl.when(z > 1)
         def _():
             p2out[r] = mm(gp[r], w[2], NT).astype(BF16)
             p2_copy[j].start()
 
+        if j >= OWE_LAG:
+            owe_next(j - OWE_LAG)
+
     sigt[1] = sig1[...].T
     sigt[2] = sig2[...].T
 
-    order = (3, 0, 2, 1)
     conv_cols = 2 * chans // PIECES
     proj_cols = chans // PIECES
+    sub = part // HALVES
     c_copy, x_copy = {}, {}
-    for q in order:
+
+    def weight_grads(q):
         for k in range(TAPS):
             grads[q, :, k * conv_cols:(k + 1) * conv_cols] = mm(
                 sigt[k], gp[:, q * conv_cols:(q + 1) * conv_cols]
@@ -212,7 +239,7 @@
         grads[q, :, TAPS * conv_cols:] = mm(
             gatedt[...], cot[:, q * proj_cols:(q + 1) * proj_cols]
         ).astype(BF16)
-        for o in range(nx):
+        for o in list(range(1, nx)) + [0]:
             e = lax.rem(d + o, nx)
             theirs = pl.ds(pl.multiple_of((e * nc + 1 - c) * part, 16), part)
             c_copy[q, o] = copy(
@@ -220,7 +247,7 @@
             )
             c_copy[q, o].start()
 
-    for q in order:
+    def sum_pair(q):
         for o in list(range(1, nx)) + [0]:
             c_copy[q, o].wait_recv()
             e = lax.rem(d + o, nx)
@@ -230,40 +257,41 @@
                 share[q] = summed
             else:
                 x_out[q, o] = summed.astype(BF16)
-                x_copy[q, o] = copy(
-                    x_out.at[q, o], x_in.at[q, o], x_s.at[q, o], x_r.at[q, o], dp=e
-                )
-                x_copy[q, o].start()
-
-    for j in range(CHUNKS):
-        r = rows_of(j)
-
-        @pl.when(above)
-        def _():
-            p2_copy[j].wait_recv()
-
-        @pl.when(below)
-        def _():
-            p1out[r] = (mm(gp[r], w[1], NT) + p2in[r].astype(F32)).astype(BF16)
-            p1_copy[j].start()
-
+                for f in range(HALVES):
+                    at = pl.ds(f * sub, sub)
+                    x_copy[q, o, f] = copy(
+                        x_out.at[q, o, at], x_in.at[q, o, at],
+                        x_s.at[q, o, f], x_r.at[q, o, f], dp=e,
+                    )
+                    x_copy[q, o, f].start()
+
+    for q in range(PIECES):
+        weight_grads(q)
+        if q > 0:
+            sum_pair(q - 1)
+    sum_pair(PIECES - 1)
+    for j in range(CHUNKS - OWE_LAG, CHUNKS):
+        owe_next(j)
     for j in range(CHUNKS):
         r = rows_of(j)
         out[r] = (sig[r].astype(F32) + mm(gated[r], wp[...])).astype(BF16)
-    for j in range(CHUNKS):
-        r = rows_of(j)
-        local_sum = cot[r].astype(F32) + mm(gp[r], w[0], NT)
-
-        @pl.when(above)
-        def _():
-            p1_copy[j].wait_recv()
-
-        gin[r] = (local_sum + p1in[r].astype(F32)).astype(BF16)
-
-    def take_x(q):
+        gin_sum[r] = cot[r].astype(F32) + mm(gp[r], w[0], NT)
+
+    def take_x(q, f):
+        at = pl.ds(f * sub, sub)
         for o in range(1, nx):
-            x_copy[q, o].wait_recv()
-            share[q] += x_in[q, o].astype(F32)
+            x_copy[q, o, f].wait_recv()
+            share[q, at] += x_in[q, o, at].astype(F32)
+
+    def finish_input():
+        for j in range(CHUNKS):
+            r = rows_of(j)
+
+            @pl.when(above)
+            def _():
+                p1_copy[j].wait_recv()
+
+            gin[r] = (gin_sum[r] + p1in[r].astype(F32)).astype(BF16)
 
     def write_out(q, values):
         for k in range(TAPS):
@@ -273,116 +301,128 @@
         gproj[:, q * proj_cols:(q + 1) * proj_cols] = values[:, TAPS * conv_cols:]
 
     if reduce_time:
-        up = [
-            copy(z_out.at[q], z_below.at[q], zb_s.at[q], zb_r.at[q], seq=z + 1)
-            for q in range(PIECES)
-        ]
-        down = [
-            copy(z_out.at[q], z_above.at[q], za_s.at[q], za_r.at[q], seq=z - 1)
-            for q in range(PIECES)
-        ]
-
-        def send_up(q):
-            @pl.when(z < q)
-            def _():
-                @pl.when(below)
-                def _():
-                    up[q].wait_recv()
-                    z_out[q] = (share[q] + z_below[q].astype(F32)).astype(BF16)
-
+        units = [(q, f) for q in range(PIECES) for f in range(HALVES)]
+
+        def unit(ref, q, f):
+            return ref.at[q, pl.ds(f * sub, sub)]
+
+        def up(q, f):
+            return copy(
+                unit(z_out, q, f), unit(z_below, q, f), zb_s.at[q, f], zb_r.at[q, f], seq=z + 1
+            )
+
+        def down(q, f):
+            return copy(
+                unit(z_out, q, f), unit(z_above, q, f), za_s.at[q, f], za_r.at[q, f], seq=z - 1
+            )
+
+        def total_up(q, f):
+            return copy(
+                unit(total, q, f), unit(total, q, f), tu_s.at[q, f], t_r.at[q, f], seq=z + 1
+            )
+
+        def total_down(q, f):
+            return copy(
+                unit(total, q, f), unit(total, q, f), td_s.at[q, f], t_r.at[q, f], seq=z - 1
+            )
+
+        def gather_in(q, f):
+            at = pl.ds(f * sub, sub)
+            owner = 2
+            take_x(q, f)
+
+            @pl.when((z < owner) & below)
+            def _():
+                up(q, f).wait_recv()
+                share[q, at] += z_below[q, at].astype(F32)
+
+            @pl.when((z > owner) & above)
+            def _():
+                down(q, f).wait_recv()
+                share[q, at] += z_above[q, at].astype(F32)
+
+            @pl.when(z != owner)
+            def _():
+                z_out[q, at] = share[q, at].astype(BF16)
+
+            @pl.when(z < owner)
+            def _():
+                up(q, f).start()
+
+            @pl.when(z > owner)
+            def _():
+                down(q, f).start()
+
+        def finish_total(q, f):
+            at = pl.ds(f * sub, sub)
+
+            @pl.when(z == 2)
+            def _():
+                up(q, f).wait_recv()
+                down(q, f).wait_recv()
+                total[q, at] = (
+                    share[q, at] + z_below[q, at].astype(F32) + z_above[q, at].astype(F32)
+                ).astype(BF16)
+                total_up(q, f).start()
+                total_down(q, f).start()
+
+        def hand_on(q, f):
+            owner = 2
+
+            @pl.when((z < owner) & below)
+            def _():
+                total_down(q, f).wait_recv()
+                total_down(q, f).start()
+
+            @pl.when((z > owner) & above)
+            def _():
+                total_up(q, f).wait_recv()
+                total_up(q, f).start()
+
+        for i in range(len(units) + LAG_ON):
+            if i < len(units):
+                gather_in(*units[i])
+            if 0 <= i - LAG_TOTAL < len(units):
+                finish_total(*units[i - LAG_TOTAL])
+            if 0 <= i - LAG_ON < len(units):
+                hand_on(*units[i - LAG_ON])
+
+        finish_input()
+        for q in range(PIECES):
+            for f in range(HALVES):
                 @pl.when(z == 0)
                 def _():
-                    z_out[q] = share[q].astype(BF16)
-
-                up[q].start()
-
-        def send_down(q):
-            @pl.when(z > q)
-            def _():
-                @pl.when(above)
-                def _():
-                    down[q].wait_recv()
-                    z_out[q] = (share[q] + z_above[q].astype(F32)).astype(BF16)
+                    total_down(q, f).wait_recv()
 
                 @pl.when(z == nz - 1)
                 def _():
-                    z_out[q] = share[q].astype(BF16)
-
-                down[q].start()
-
-        take_x(3)
-        send_up(3)
-        take_x(0)
-        send_down(0)
-        take_x(2)
-        send_up(2)
-        take_x(1)
-        send_down(1)
-        send_up(1)
-        send_down(2)
-
-        def total_up(q):
-            return copy(total.at[q], total.at[q], tu_s.at[q], t_r.at[q], seq=z + 1)
-
-        def total_down(q):
-            return copy(total.at[q], total.at[q], td_s.at[q], t_r.at[q], seq=z - 1)
-
+                    total_up(q, f).wait_recv()
+
+            write_out(q, total[q].astype(F32) * factor)
+
+        for q, f in units:
+            owner = 2
+
+            @pl.when(z < owner)
+            def _():
+                up(q, f).wait_send()
+
+            @pl.when(z > owner)
+            def _():
+                down(q, f).wait_send()
+
+            @pl.when((z >= owner) & above)
+            def _():
+                total_up(q, f).wait_send()
+
+            @pl.when((z <= owner) & below)
+            def _():
+                total_down(q, f).wait_send()
+    else:
+        finish_input()
         for q in range(PIECES):
-            @pl.when(z == q)
-            def _():
-                if q > 0:
-                    up[q].wait_recv()
-                    share[q] += z_below[q].astype(F32)
-                if q < nz - 1:
-                    down[q].wait_recv()
-                    share[q] += z_above[q].astype(F32)
-                total[q] = share[q].astype(BF16)
-                if q < nz - 1:
-                    total_up(q).start()
-                if q > 0:
-                    total_down(q).start()
-
-        for distance in range(1, nz):
-            @pl.when(z >= distance)
-            def _():
-                q = z - distance
-                total_up(q).wait_recv()
-
-                @pl.when(above)
-                def _():
-                    total_up(q).start()
-
-            @pl.when(z + distance <= nz - 1)
-            def _():
-                q = z + distance
-                total_down(q).wait_recv()
-
-                @pl.when(below)
-                def _():
-                    total_down(q).start()
-
-        for q in range(PIECES):
-            write_out(q, total[q].astype(F32) * factor)
-
-        for q in range(PIECES):
-            @pl.when(z < q)
-            def _():
-                up[q].wait_send()
-
-            @pl.when(z > q)
-            def _():
-                down[q].wait_send()
-
-            @pl.when((z >= q) & above)
-            def _():
-                total_up(q).wait_send()
-
-            @pl.when((z <= q) & below)
-            def _():
-                total_down(q).wait_send()
-    else:
-        for q in order:
-            take_x(q)
+            for f in range(HALVES):
+                take_x(q, f)
             write_out(q, share[q])
 
     for item in (
@@ -404,8 +444,12 @@
     @pl.when(below)
     def _():
         for j in range(CHUNKS):
+            p1_copy[j].wait_send()
+
+    @pl.when(z > 1)
+    def _():
+        for j in range(CHUNKS):
             p2_copy[j].wait_send()
-            p1_copy[j].wait_send()
 
 
 def local(sizes, signal, conv_weight, proj_weight, cotangent):
@@ -420,7 +464,7 @@
     block = vmem((rows, chans), BF16)
     piece = vmem((PIECES, part, width), BF16)
     scratch = [
-        block, block,
+        block, block, vmem((rows, chans), F32), block, block,
         vmem((TAPS, chans, rows), BF16), vmem((chans, rows), BF16),
         vmem((TAPS, chans, 2 * chans), BF16), block, vmem((rows, 2 * chans), BF16), block,
         block, block, block, block,
@@ -431,8 +475,10 @@
         vmem((PIECES, part, width), F32),
         piece, piece, piece, piece,
     ] + [dma((2, CHUNKS))] * 2 + [dma((TAPS + 1, nx))] * 4 + [dma((TAPS + 1, nx, 2))] * 2 \
-        + [dma((2, CHUNKS))] * 2 + [dma((PIECES, nx))] * 4 + [dma((PIECES,))] * 7
+        + [dma((2, CHUNKS))] * 2 + [dma((PIECES, nx))] * 2 + [dma((PIECES, nx, HALVES))] * 2 \
+        + [dma((PIECES, HALVES))] * 7 + [dma((4,))]
     spec = pl.BlockSpec(memory_space=pltpu.VMEM)
+    anywhere = pl.BlockSpec(memory_space=pl.ANY)
     output, grad_input, conv, proj = pl.pallas_call(
         functools.partial(layer_kernel, sizes, factor),
         out_shape=(
@@ -441,11 +487,11 @@
             jax.ShapeDtypeStruct((TAPS, part, 2 * chans), F32),
             jax.ShapeDtypeStruct((part, chans), F32),
         ),
-        in_specs=[spec] * 4,
+        in_specs=[anywhere] * 4,
         out_specs=(spec,) * 4,
         scratch_shapes=scratch,
         compiler_params=pltpu.CompilerParams(
-            collective_id=0, has_side_effects=True, vmem_limit_bytes=48 * 1024 * 1024
+            collective_id=0, has_side_effects=True, vmem_limit_bytes=56 * 1024 * 1024
         ),
         cost_estimate=pl.CostEstimate(
             flops=22 * rows * chans * chans, bytes_accessed=8 << 20, transcendentals=2 * rows * chans

time: 101 us -> 85.2 us (0.84)
  Pallas kernels: 92.5 us -> 78.7 us
  local copies, waits for them, and re-layouts: 7.54 us -> 5.71 us
    pallas_call x1, Pallas kernels: 92.5 us -> 78.7 us  [local(): pl.pallas_call(functools.partial(layer_kernel, sizes, factor), out_shape=...]
    unnamed x12 -> x8, local copies, waits for them, and re-layouts: 7.54 us -> 5.71 us
where the time goes in v2:
time: 85.2 us; the launch traced here: 85 us
  Pallas kernels  78.7 us (92%)
  local copies, waits for them, and re-layouts  5.71 us (7%)
    pallas_call x1, Pallas kernels, local(): pl.pallas_call(functools.partial(layer_kernel, sizes, factor), out_shape=...  78.7 us
    unnamed x8, local copies, waits for them, and re-layouts  5.71 us

profile of v2, /device:TPU:0, one launch (start us, length us, event | category | flops | bytes accessed | tf_op | source)
XLA Modules:
  0.0 85.0 jit_solution(18128635445907160811)
XLA Ops:
  0.6 78.7 %shard_map.75 = (bf16[512,512]{1,0:T(8,128)(2,1)}, bf16[512,512]{1,0:T(8,128)(2,1)}, f32[3,128,1024]{2,1,0:T(8,128)}, f32[128,512]{1,0:T(8,128)}) custom-call(bf16[512,512]{1,0:T(8,128)(2,1)} %bitcast.10, bf16[3,128,1024]{2,1,0:T(8,128)(2,1)} %bitcast.9, bf16[128,512]{1,0:T(8,128)(2,1)} %pw.1, bf16[512,512]{1,0:T(8,128)(2,1)} %bitcast.11), custom_call_target="tpu_custom_call" | custom-call | flops 2952790016 | bytes 8388608 | tf_op jit(solution)/shard_map/pallas_call | solution.py:482
  79.3 0.0 copy-start
  79.3 2.0 %copy.12 = bf16[1,512,512]{2,1,0:T(8,128)(2,1)} copy(bf16[1,512,512]{2,1,0:T(8,128)(2,1)} %bitcast.8) | data formatting | bytes 1048576
  81.3 1.9 %copy.13 = bf16[1,512,512]{2,1,0:T(8,128)(2,1)} copy(bf16[1,512,512]{2,1,0:T(8,128)(2,1)} %bitcast.7) | data formatting | bytes 1048576
  83.2 0.0 copy-done
  83.2 0.0 copy-start.1
  83.2 1.1 %copy.14 = f32[128,3,1024]{2,0,1:T(8,128)} copy(f32[128,3,1024]{2,0,1:T(8,128)S(1)} %bitcast.6) | data formatting | bytes 3145728
  84.3 0.0 copy-done.1
  84.3 0.7 copy.15
Async XLA Ops:
  79.3 3.9 %copy-start = (f32[3,128,1024]{2,1,0:T(8,128)S(1)}, f32[3,128,1024]{2,1,0:T(8,128)}, u32[]{:S(2)}) copy-start(f32[3,128,1024]{2,1,0:T(8,128)} %get-tuple-element.10) | copy-start | bytes 4718596
  83.2 1.1 %copy-start.1 = (f32[128,512]{1,0:T(8,128)S(1)}, f32[128,512]{1,0:T(8,128)}, u32[]{:S(2)}) copy-start(f32[128,512]{1,0:T(8,128)} %get-tuple-element.19) | copy-start | bytes 786436
